TPU v7x, 512 devices: a whole 4x4x16 slice. The times are simulated.
512 devices in a mesh: row: 64 (over y, z_hi, x, core), col: 8 (over z_lo).
Axes of the slice: x: 4, y: 4, z: 16 (z_hi: 2, z_lo: 8; z = z_hi * 8 + z_lo), core: 2. Of those that a mesh axis runs over, the one named last changes fastest.
Arguments:
- queries: bfloat16 [8192, 8192], P('row'), may hold values from -18 to 18
- keys: bfloat16 [8192, 512], P(('row', 'col')), may hold values from -18 to 18
- values: bfloat16 [8192, 512], P(('row', 'col')), may hold values from -6 to 6
- order: int32 [8192], P(('row', 'col')), may hold values from 0 to 8191, as said below
Outputs:
- attended: bfloat16 [8192, 8192], P(('row', 'col'))
Inputs may be any that keep to these rules, and one draw needn't show every extreme that they name: `order`: each device's 16 entries are consecutive increasing positions; every position of the sequence appears once.
All inputs are finite; a program needn't handle non-finite values.
Results may differ from a plain program's by a relative error of at most 0.03.
Values may be sent and summed in bfloat16 or wider, within the bound.
A program may use at most 64 MiB of HBM per device.

v0:
```python
import math

import jax
import jax.numpy as jnp
from jax import lax
from jax.experimental import pallas as pl
from jax.experimental.pallas import tpu as pltpu
from jax.sharding import PartitionSpec as P

HD = 128
KVH = 4
GROUP = 16
TOK = 16
NX, NY, NZ, NLO = 4, 4, 16, 8
QTOK = 64
WIDTH = GROUP * HD
HALF = 8
BKEYS = HALF * TOK
BLOCK = BKEYS + HD + TOK
KEYS = 2 * BKEYS
ROWS = 8
BF = jnp.bfloat16
F32 = jnp.float32
MASKED = -1e30
RATE = math.log2(math.e) / math.sqrt(HD)

ORDER = [
    (0, 0, 0), (1, 0, 0), (3, 0, 0), (0, 3, 0), (0, 0, 1), (1, 3, 0), (0, 1, 0), (3, 3, 0),
    (2, 0, 0), (1, 1, 0), (3, 0, 1), (3, 1, 0), (0, 3, 1), (0, 1, 1), (1, 0, 1), (2, 3, 0),
    (0, 2, 0), (2, 0, 1), (3, 3, 1), (2, 1, 0), (0, 2, 1), (3, 1, 1), (1, 3, 1), (1, 2, 0),
    (3, 2, 0), (2, 3, 1), (1, 1, 1), (3, 2, 1), (2, 1, 1), (1, 2, 1), (2, 2, 0), (2, 2, 1),
]
HELD = [
    4, 4, 6, 6, 10, 10, 11, 11, 12, 12,
    14, 16, 16, 16, 18, 18, 20, 20, 24, 24,
    24, 26, 26, 26, 28, 28, 30, 30, 32, 32,
]
BLOCKS = len(ORDER)
SLOT = {place: index for index, place in enumerate(ORDER)}
STEP = {"A-": (1, 0), "A+": (-1, 0), "B-": (0, 1), "B+": (0, -1)}


def onward(a, b, wave):
    ways = []
    if b == 0:
        if a == 0:
            ways += ["A-", "A+"]
        if (a, wave) == (1, 0):
            ways.append("A-")
        if (a, wave) == (3, 1):
            ways.append("A+")
        ways += ["B-", "B+"]
    if (b, wave) == (1, 0):
        ways.append("B-")
    if (b, wave) == (3, 1):
        ways.append("B+")
    return ways


ROUTES = []
for place in ORDER:
    for way in onward(*place):
        da, db = STEP[way]
        there = ((place[0] + da) % 4, (place[1] + db) % 4, place[2])
        ROUTES.append((SLOT[place], way, SLOT[there]))


def kernel(
    q_hbm, k_hbm, v_hbm, order_hbm, out_ref,
    mine, stage, landed, order_own, pos_own, pos_line, q_raw, q_pos, q_t,
    even, odd, peak_even, peak_odd, acc, top, half_send, half_recv, stat_send, stat_recv, out_stage,
    q_sem, kv_sem, order_sem,
    z_send, z_recv, p_send, p_recv, f_send, m_recv, t_send, t_recv, h_send, h_recv, o_send, o_recv,
):
    row = lax.axis_index("row")
    col = lax.axis_index("col")
    core = row % 2
    x = (row // 2) % NX
    y = row // (4 * NX)
    z = ((row // (2 * NX)) % 2) * NLO + col
    head = col % KVH
    half = col // KVH

    order_copy = pltpu.make_async_copy(order_hbm, order_own, order_sem)
    order_copy.start()
    for g in range(KVH):
        columns = slice(g * HD, (g + 1) * HD)
        pltpu.make_async_copy(k_hbm.at[:, columns], stage.at[g, 0], kv_sem).start()
        pltpu.make_async_copy(v_hbm.at[:, columns], stage.at[g, 1], kv_sem).start()
    q_copy = pltpu.make_async_copy(
        q_hbm.at[pl.ds(half * QTOK, QTOK), pl.ds(pl.multiple_of(head * WIDTH, WIDTH), WIDTH)],
        q_raw.at[0], q_sem,
    )
    q_copy.start()

    def device(x_at, y_at, z_at, core_at):
        return (y_at * (4 * NX) + (z_at // NLO) * (2 * NX) + x_at * 2 + core_at, z_at % NLO)

    line = [None] + [device(x, y, (z + d) % NZ, core) for d in range(1, NZ)]
    plane = {}
    for way, (da, db) in STEP.items():
        sx = (1 - core) * da + core * db
        sy = core * da + (1 - core) * db
        plane[way] = device((x - sx + NX) % NX, (y - sy + NY) % NY, z, core)
    twin = device(x, y, z, 1 - core)

    barrier = pltpu.get_barrier_semaphore()
    others = line[1:] + list(plane.values()) + [twin]
    for other in others:
        pl.semaphore_signal(barrier, inc=1, device_id=other, device_id_type=pl.DeviceIdType.MESH)

    order_copy.wait()
    pos_own[...] = jnp.full((1, 128), order_own[0], jnp.int32)
    pltpu.make_async_copy(stage, stage, kv_sem).wait()
    pl.semaphore_wait(barrier, len(others))

    def remote(src, dst, send, recv, to):
        return pltpu.make_async_remote_copy(
            src_ref=src, dst_ref=dst, send_sem=send, recv_sem=recv,
            device_id=to, device_id_type=pl.DeviceIdType.MESH,
        )

    line_copies = []
    for wave, ds in enumerate(([12, 13, 3, 14, 2, 15, 1], [8, 7, 9, 6, 10, 5, 11, 4])):
        for d in ds:
            at = wave * HALF + (NZ - d) % HALF
            line_copies.append(remote(
                stage.at[(z + d) % KVH], landed.at[at], z_send.at[d - 1], z_recv.at[wave], line[d]
            ))
            line_copies.append(remote(
                pos_own, pos_line.at[at], p_send.at[d - 1], p_recv.at[wave], line[d]
            ))
    for copy in line_copies:
        copy.start()
    landed[0] = stage[head]
    pos_line[0] = pos_own[...]

    q_copy.wait()
    q_over = remote(q_raw.at[0], q_raw.at[1], t_send.at[0], t_recv.at[0], twin)
    q_over.start()

    def turn(side):
        for cc in range(4):
            rows = jnp.concatenate(
                [
                    q_raw[side, cc * TOK:(cc + 1) * TOK, g * HD:(g + 1) * HD]
                    for g in range(GROUP)
                ],
                axis=0,
            )
            token = lax.broadcasted_iota(jnp.int32, (HD, 256), 0)
            lane = lax.broadcasted_iota(jnp.int32, (HD, 256), 1)
            q_t[side * 4 + cc, 0:HD] = rows.T
            q_t[side * 4 + cc, HD:] = jnp.where(
                token == side * QTOK + cc * TOK + lane % TOK, 1.0, 0.0
            ).astype(BF)

    turn(0)
    q_over.wait_recv()
    turn(1)
    acc[...] = jnp.zeros_like(acc)
    top[...] = jnp.full_like(top, MASKED)

    lane16 = lax.broadcasted_iota(jnp.int32, (TOK, 128), 1)

    def collect(wave):
        first = 1 - wave
        got = pos_line.at[pl.ds(wave * HALF + first, HALF - first)]
        pltpu.make_async_copy(got, got, p_recv.at[wave]).wait()
        got = landed.at[pl.ds(wave * HALF + first, HALF - first)]
        pltpu.make_async_copy(got, got, z_recv.at[wave]).wait()
        slot = SLOT[(0, 0, wave)]
        places = [wave * HALF + d for d in range(HALF)]
        starts = jnp.concatenate([pos_line[d] for d in places * 2], axis=0)
        mine[slot, BKEYS + HD:] = jnp.where(
            lane16 < 64, starts // 128, starts % 128
        ).astype(F32).astype(BF)
        for d in range(HALF):
            mine[slot, d * TOK:(d + 1) * TOK] = landed[wave * HALF + d, 0]
        mine[slot, BKEYS:BKEYS + HD] = jnp.concatenate([landed[d, 1] for d in places], axis=0).T

    def route(n):
        slot, way, there = ROUTES[n]
        return remote(mine.at[slot], mine.at[there], f_send.at[n], m_recv.at[there], plane[way])

    def wait_mine(slot):
        pltpu.make_async_copy(mine.at[slot], mine.at[slot], m_recv.at[slot]).wait()

    def pass_on(slot):
        for n in range(len(ROUTES)):
            if ROUTES[n][0] == slot:
                route(n).start()

    collect(0)
    pass_on(0)

    lane1 = lax.broadcasted_iota(jnp.int32, (1, 128), 1)
    token_pos = jnp.zeros((1, 128), jnp.int32)
    for cc in range(4):
        token_pos = jnp.where(
            (lane1 % QTOK) // TOK == cc,
            pos_line[(cc - head + HALF) % HALF] + lane1 % TOK, token_pos,
        )
    q_pos[0] = token_pos
    pos_over = remote(q_pos.at[0], q_pos.at[1], t_send.at[1], t_recv.at[1], twin)
    pos_over.start()

    def receive(first, last):
        for slot in range(first, last):
            if slot == SLOT[(0, 0, 1)]:
                collect(1)
            else:
                wait_mine(slot)
            pass_on(slot)

    early = max(2, HELD[0] - 2)
    receive(1, early)
    pos_over.wait_recv()
    limit = (
        jnp.where(lane1 < QTOK, q_pos[0], q_pos[1]) - lax.broadcasted_iota(jnp.int32, (TOK, 128), 0)
    ).astype(F32)

    def augmented(slot):
        word = mine[slot, BKEYS + HD:].astype(F32)
        turned = pltpu.roll(word, 64, 1)
        start = jnp.where(lane16 < 64, word * 128.0 + turned, turned * 128.0 + word)
        bias = jnp.concatenate(
            [jnp.where(start[d:d + 1, :] <= limit, 0.0, MASKED).astype(BF) for d in range(HALF)],
            axis=0,
        )
        return jnp.concatenate([mine[slot, 0:BKEYS], bias], axis=1)

    def keys_of(s):
        return jnp.concatenate([augmented(2 * s), augmented(2 * s + 1)], axis=0)

    def values_of(s):
        parts = [mine[2 * s + k, BKEYS:BKEYS + HD] for k in (0, 1)]
        return jnp.concatenate(
            [jnp.concatenate(parts, axis=1), jnp.ones((TOK, KEYS), BF)], axis=0
        )

    def score(cc, keys, into, peak):
        scores = jnp.dot(keys, q_t[cc], preferred_element_type=F32)
        into[cc] = scores
        peak[cc] = jnp.max(scores, axis=0, keepdims=True)

    def absorb(cc, values, source, peak):
        old = top[cc]
        new = jnp.maximum(old, peak[cc])
        probs = jnp.exp2((source[cc] - new) * RATE).astype(BF)
        acc[cc] = acc[cc] * jnp.exp2((old - new) * RATE) + jnp.dot(
            values, probs, preferred_element_type=F32
        )
        top[cc] = new

    def step(s, source, peak, into, into_peak, between):
        for part in range(2):
            between(part)
            if part == 0:
                keys = keys_of(s + 1)
                values = values_of(s)
            for cc in range(4 * part, 4 * part + 4):
                score(cc, keys, into, into_peak)
                absorb(cc, values, source, peak)

    keys = keys_of(0)
    for cc in range(ROWS):
        score(cc, keys, even, peak_even)
    held = [early] + HELD
    step(
        0, even, peak_even, odd, peak_odd, lambda part: receive(held[part], held[part + 1])
    )

    def pair(i, carry):
        for k in range(2):
            def between(part):
                for v in range(7):
                    at = 2 * (2 * v + 1 + k) + part
                    if held[at] < held[at + 1]:
                        @pl.when(i == v)
                        def _():
                            receive(held[at], held[at + 1])

            s = 2 * i + 1 + k
            if k == 0:
                step(s, odd, peak_odd, even, peak_even, between)
            else:
                step(s, even, peak_even, odd, peak_odd, between)
        return carry

    lax.fori_loop(0, 7, pair, 0)

    values = values_of(15)
    over = []
    for cc in range(4):
        absorb(4 + cc, values, odd, peak_odd)
        half_send[cc] = acc[4 + cc, 0:HD].astype(BF)
        stat_send[2 * cc] = acc[4 + cc, HD:HD + 1]
        stat_send[2 * cc + 1] = top[4 + cc]
        over.append((
            remote(half_send.at[cc], half_recv.at[cc], h_send.at[2 * cc], h_recv.at[2 * cc], twin),
            remote(
                stat_send.at[pl.ds(2 * cc, 2)], stat_recv.at[pl.ds(2 * cc, 2)],
                h_send.at[2 * cc + 1], h_recv.at[2 * cc + 1], twin,
            ),
        ))
        for copy in over[-1]:
            copy.start()
    for cc in range(4):
        absorb(cc, values, odd, peak_odd)

    columns = pl.ds(pl.multiple_of(head * WIDTH, WIDTH), WIDTH)
    out_copies = []
    for j in (2, 1, 3, 0):
        cc = (head + j) % KVH
        for kind, (sent, got) in enumerate((
            (half_send.at[cc], half_recv.at[cc]),
            (stat_send.at[pl.ds(2 * cc, 2)], stat_recv.at[pl.ds(2 * cc, 2)]),
        )):
            remote(sent, got, h_send.at[2 * cc + kind], h_recv.at[2 * cc + kind], twin).wait_recv()
        own = top[cc]
        other = stat_recv[2 * cc + 1]
        new = jnp.maximum(own, other)
        own_part = jnp.exp2((own - new) * RATE)
        other_part = jnp.exp2((other - new) * RATE)
        total = acc[cc, HD:HD + 1] * own_part + stat_recv[2 * cc] * other_part
        own_part = own_part / total
        other_part = other_part / total
        done = (acc[cc, 0:HD] * own_part + half_recv[cc].astype(F32) * other_part).T.astype(BF)
        for g in range(GROUP):
            out_stage[j, :, g * HD:(g + 1) * HD] = done[g * TOK:(g + 1) * TOK, :]
        if j == 0:
            out_copies.append(pltpu.make_async_copy(
                out_stage.at[j], out_ref.at[:, columns], o_send.at[j]
            ))
        else:
            to = device(x, y, (z // KVH) * KVH + cc, core)
            out_copies.append(remote(
                out_stage.at[j], out_ref.at[:, columns], o_send.at[j], o_recv.at[j], to
            ))
        out_copies[-1].start()
    for copy in line_copies:
        copy.wait_send()
    for n in range(len(ROUTES)):
        route(n).wait_send()
    q_over.wait_send()
    pos_over.wait_send()
    for copies in over:
        for copy in copies:
            copy.wait_send()
    for j in (1, 2, 3):
        source = (head - j + KVH) % KVH
        place = out_ref.at[:, pl.ds(pl.multiple_of(source * WIDTH, WIDTH), WIDTH)]
        pltpu.make_async_copy(place, place, o_recv.at[j]).wait()
    for copy in out_copies[:3]:
        copy.wait_send()
    out_copies[3].wait()


def shards(queries, keys, values, order):
    dma = pltpu.SemaphoreType.DMA
    return pl.pallas_call(
        kernel,
        out_shape=jax.ShapeDtypeStruct((TOK, KVH * WIDTH), BF),
        in_specs=[pl.BlockSpec(memory_space=pl.ANY)] * 4,
        out_specs=pl.BlockSpec(memory_space=pl.ANY),
        scratch_shapes=[
            pltpu.VMEM((BLOCKS, BLOCK, HD), BF),
            pltpu.VMEM((KVH, 2, TOK, HD), BF),
            pltpu.VMEM((NZ, 2, TOK, HD), BF),
            pltpu.SMEM((TOK,), jnp.int32),
            pltpu.VMEM((1, 128), jnp.int32),
            pltpu.VMEM((NZ, 1, 128), jnp.int32),
            pltpu.VMEM((2, QTOK, WIDTH), BF),
            pltpu.VMEM((2, 1, 128), jnp.int32),
            pltpu.VMEM((ROWS, 2 * HD, 256), BF),
            pltpu.VMEM((ROWS, KEYS, 256), F32),
            pltpu.VMEM((ROWS, KEYS, 256), F32),
            pltpu.VMEM((ROWS, 1, 256), F32),
            pltpu.VMEM((ROWS, 1, 256), F32),
            pltpu.VMEM((ROWS, HD + TOK, 256), F32),
            pltpu.VMEM((ROWS, 1, 256), F32),
            pltpu.VMEM((4, HD, 256), BF),
            pltpu.VMEM((4, HD, 256), BF),
            pltpu.VMEM((8, 1, 256), F32),
            pltpu.VMEM((8, 1, 256), F32),
            pltpu.VMEM((4, TOK, WIDTH), BF),
            dma, dma, dma,
            dma((NZ - 1,)), dma((2,)), dma((NZ - 1,)), dma((2,)),
            dma((len(ROUTES),)), dma((BLOCKS,)), dma((2,)), dma((2,)),
            dma((8,)), dma((8,)), dma((4,)), dma((4,)),
        ],
        compiler_params=pltpu.CompilerParams(
            collective_id=0, has_side_effects=True, vmem_limit_bytes=60 * 1024 * 1024
        ),
        cost_estimate=pl.CostEstimate(
            flops=4 * 1024 * 8192 * 128, bytes_accessed=1 << 20, transcendentals=1024 * 8192
        ),
    )(queries, keys, values, order)


def solution(mesh):
    return jax.shard_map(
        shards,
        mesh=mesh,
        in_specs=(
            P("row", None),
            P(("row", "col"), None),
            P(("row", "col"), None),
            P(("row", "col")),
        ),
        out_specs=P(("row", "col"), None),
        check_vma=False,
    )
```

profile of v0, /device:TPU:1, one launch (start us, length us, event | category | flops | bytes accessed | tf_op | source)
XLA Modules:
  0.0 54.9 jit_solution(700261957931295694)
XLA Ops:
  0.0 53.2 %shard_map.46 = bf16[16,8192]{1,0:T(8,128)(2,1)} custom-call(bf16[128,8192]{1,0:T(8,128)(2,1)} %q_hbm.1, bf16[16,512]{1,0:T(8,128)(2,1)} %k_hbm.1, bf16[16,512]{1,0:T(8,128)(2,1)} %v_hbm.1, s32[16]{0:T(128)} %order_hbm.1), custom_call_target="tpu_custom_call" | custom-call | flops 4294967296 | bytes 1048576 | tf_op jit(solution)/shard_map/pallas_call | solution.py:362
  53.2 1.7 %copy.6 = bf16[16,8192]{1,0:T(8,128)(2,1)} copy(bf16[16,8192]{1,0:T(8,128)(2,1)} %shard_map.46) | data formatting | bytes 524288
where the time goes:
time: 55 us; the launch traced here: 54.9 us
  Pallas kernels  53.2 us (97%)
  local copies, waits for them, and re-layouts  1.67 us (3%)
    pallas_call x1, Pallas kernels, shards(): pl.pallas_call(kernel, out_shape=jax.ShapeDtypeStruct((TOK, KVH * WIDTH),...  53.2 us
    unnamed x1, local copies, waits for them, and re-layouts  1.67 us

commit v1 on v0

--- a/solution.py
+++ b/solution.py
@@ -67,7 +67,7 @@
 
 def kernel(
     q_hbm, k_hbm, v_hbm, order_hbm, out_ref,
-    mine, stage, landed, order_own, pos_own, pos_line, q_raw, q_pos, q_t,
+    mine, kv_own, stage, landed, order_own, pos_own, pos_line, q_raw, q_pos, q_t,
     even, odd, peak_even, peak_odd, acc, top, half_send, half_recv, stat_send, stat_recv, out_stage,
     q_sem, kv_sem, order_sem,
     z_send, z_recv, p_send, p_recv, f_send, m_recv, t_send, t_recv, h_send, h_recv, o_send, o_recv,
@@ -83,10 +83,12 @@
 
     order_copy = pltpu.make_async_copy(order_hbm, order_own, order_sem)
     order_copy.start()
-    for g in range(KVH):
-        columns = slice(g * HD, (g + 1) * HD)
-        pltpu.make_async_copy(k_hbm.at[:, columns], stage.at[g, 0], kv_sem).start()
-        pltpu.make_async_copy(v_hbm.at[:, columns], stage.at[g, 1], kv_sem).start()
+    fetches = [
+        pltpu.make_async_copy(array, kv_own.at[n], kv_sem.at[n])
+        for n, array in enumerate((k_hbm, v_hbm))
+    ]
+    for fetch in fetches:
+        fetch.start()
     q_copy = pltpu.make_async_copy(
         q_hbm.at[pl.ds(half * QTOK, QTOK), pl.ds(pl.multiple_of(head * WIDTH, WIDTH), WIDTH)],
         q_raw.at[0], q_sem,
@@ -111,7 +113,10 @@
 
     order_copy.wait()
     pos_own[...] = jnp.full((1, 128), order_own[0], jnp.int32)
-    pltpu.make_async_copy(stage, stage, kv_sem).wait()
+    for n, fetch in enumerate(fetches):
+        fetch.wait()
+        for g in range(KVH):
+            stage[g, n] = kv_own[n, :, g * HD:(g + 1) * HD]
     pl.semaphore_wait(barrier, len(others))
 
     def remote(src, dst, send, recv, to):
@@ -120,16 +125,29 @@
             device_id=to, device_id_type=pl.DeviceIdType.MESH,
         )
 
-    line_copies = []
-    for wave, ds in enumerate(([12, 13, 3, 14, 2, 15, 1], [8, 7, 9, 6, 10, 5, 11, 4])):
-        for d in ds:
-            at = wave * HALF + (NZ - d) % HALF
-            line_copies.append(remote(
-                stage.at[(z + d) % KVH], landed.at[at], z_send.at[d - 1], z_recv.at[wave], line[d]
-            ))
-            line_copies.append(remote(
-                pos_own, pos_line.at[at], p_send.at[d - 1], p_recv.at[wave], line[d]
-            ))
+    waves = ([12, 13, 3, 14, 2, 15, 1], [8, 7, 9, 6, 10, 5, 11, 4])
+
+    def blocks_to_line(wave):
+        return [
+            remote(
+                stage.at[(z + d) % KVH], landed.at[wave * HALF + (NZ - d) % HALF],
+                z_send.at[d - 1], z_recv.at[wave], line[d],
+            )
+            for d in waves[wave]
+        ]
+
+    def positions_to_line(wave):
+        return [
+            remote(
+                pos_own, pos_line.at[wave * HALF + (NZ - d) % HALF],
+                p_send.at[d - 1], p_recv.at[wave], line[d],
+            )
+            for d in waves[wave]
+        ]
+
+    line_copies = (
+        blocks_to_line(0) + positions_to_line(0) + positions_to_line(1) + blocks_to_line(1)
+    )
     for copy in line_copies:
         copy.start()
     landed[0] = stage[head]
@@ -357,15 +375,29 @@
     out_copies[3].wait()
 
 
+def settle(source, target, sems):
+    copies = [
+        pltpu.make_async_copy(
+            source.at[:, pl.ds(n * WIDTH, WIDTH)], target.at[:, pl.ds(n * WIDTH, WIDTH)], sems.at[n]
+        )
+        for n in range(KVH)
+    ]
+    for copy in copies:
+        copy.start()
+    for copy in copies:
+        copy.wait()
+
+
 def shards(queries, keys, values, order):
     dma = pltpu.SemaphoreType.DMA
-    return pl.pallas_call(
+    attended = pl.pallas_call(
         kernel,
         out_shape=jax.ShapeDtypeStruct((TOK, KVH * WIDTH), BF),
         in_specs=[pl.BlockSpec(memory_space=pl.ANY)] * 4,
         out_specs=pl.BlockSpec(memory_space=pl.ANY),
         scratch_shapes=[
             pltpu.VMEM((BLOCKS, BLOCK, HD), BF),
+            pltpu.VMEM((2, TOK, KVH * HD), BF),
             pltpu.VMEM((KVH, 2, TOK, HD), BF),
             pltpu.VMEM((NZ, 2, TOK, HD), BF),
             pltpu.SMEM((TOK,), jnp.int32),
@@ -385,7 +417,7 @@
             pltpu.VMEM((8, 1, 256), F32),
             pltpu.VMEM((8, 1, 256), F32),
             pltpu.VMEM((4, TOK, WIDTH), BF),
-            dma, dma, dma,
+            dma, dma((2,)), dma,
             dma((NZ - 1,)), dma((2,)), dma((NZ - 1,)), dma((2,)),
             dma((len(ROUTES),)), dma((BLOCKS,)), dma((2,)), dma((2,)),
             dma((8,)), dma((8,)), dma((4,)), dma((4,)),
@@ -397,6 +429,14 @@
             flops=4 * 1024 * 8192 * 128, bytes_accessed=1 << 20, transcendentals=1024 * 8192
         ),
     )(queries, keys, values, order)
+    return pl.pallas_call(
+        settle,
+        out_shape=jax.ShapeDtypeStruct((TOK, KVH * WIDTH), BF),
+        in_specs=[pl.BlockSpec(memory_space=pl.ANY)],
+        out_specs=pl.BlockSpec(memory_space=pl.ANY),
+        scratch_shapes=[dma((KVH,))],
+        compiler_params=pltpu.CompilerParams(vmem_limit_bytes=60 * 1024 * 1024),
+    )(attended)
 
 
 def solution(mesh):

time: 55 us -> 63.7 us (1.16)
  Pallas kernels: 53.2 us -> 63.5 us
  local copies, waits for them, and re-layouts: 1.67 us -> 0 us
    pallas_call x0 -> x1, Pallas kernels: none -> 9.08 us  [shards(): pl.pallas_call(settle, out_shape=jax.ShapeDtypeStruct((TOK, KVH * WIDTH),...]
    unnamed x1 -> x0, local copies, waits for them, and re-layouts: 1.67 us -> none
    pallas_call x1, Pallas kernels: 53.2 us -> 54.5 us  [shards(): pl.pallas_call(kernel, out_shape=jax.ShapeDtypeStruct((TOK, KVH * WIDTH),...]
where the time goes in v1:
time: 63.7 us; the launch traced here: 63.6 us
  Pallas kernels  63.5 us (100%)
    pallas_call x1, Pallas kernels, shards(): pl.pallas_call(kernel, out_shape=jax.ShapeDtypeStruct((TOK, KVH * WIDTH),...  54.5 us
    pallas_call x1, Pallas kernels, shards(): pl.pallas_call(settle, out_shape=jax.ShapeDtypeStruct((TOK, KVH * WIDTH),...  9.08 us

profile of v1, /device:TPU:1, one launch (start us, length us, event | category | flops | bytes accessed | tf_op | source)
XLA Modules:
  0.0 63.6 jit_solution(15210998942579128673)
XLA Ops:
  0.0 54.5 %shard_map.46.source = bf16[16,8192]{1,0:T(8,128)(2,1)} custom-call(bf16[128,8192]{1,0:T(8,128)(2,1)} %q_hbm.1, bf16[16,512]{1,0:T(8,128)(2,1)} %k_hbm.1, bf16[16,512]{1,0:T(8,128)(2,1)} %v_hbm.1, s32[16]{0:T(128)} %order_hbm.1), custom_call_target="tpu_custom_call" | custom-call | flops 4294967296 | bytes 1048576 | tf_op jit(solution)/shard_map/pallas_call | solution.py:393
  54.5 9.1 %shard_map.47 = bf16[16,8192]{1,0:T(8,128)(2,1)} custom-call(bf16[16,8192]{1,0:T(8,128)(2,1)} %shard_map.46.source), custom_call_target="tpu_custom_call" | custom-call | tf_op jit(solution)/shard_map/pallas_call | solution.py:432

commit v2 on v0

--- a/solution.py
+++ b/solution.py
@@ -67,10 +67,10 @@
 
 def kernel(
     q_hbm, k_hbm, v_hbm, order_hbm, out_ref,
-    mine, stage, landed, order_own, pos_own, pos_line, q_raw, q_pos, q_t,
+    mine, stage, landed, order_own, q_raw, q_pos, q_t,
     even, odd, peak_even, peak_odd, acc, top, half_send, half_recv, stat_send, stat_recv, out_stage,
     q_sem, kv_sem, order_sem,
-    z_send, z_recv, p_send, p_recv, f_send, m_recv, t_send, t_recv, h_send, h_recv, o_send, o_recv,
+    z_send, z_recv, f_send, m_recv, t_send, t_recv, h_send, h_recv, o_send, o_recv,
 ):
     row = lax.axis_index("row")
     col = lax.axis_index("col")
@@ -110,8 +110,13 @@
         pl.semaphore_signal(barrier, inc=1, device_id=other, device_id_type=pl.DeviceIdType.MESH)
 
     order_copy.wait()
-    pos_own[...] = jnp.full((1, 128), order_own[0], jnp.int32)
-    pltpu.make_async_copy(stage, stage, kv_sem).wait()
+    lane16 = lax.broadcasted_iota(jnp.int32, (TOK, 128), 1)
+    start_own = jnp.full((TOK, 128), order_own[0], jnp.int32)
+    start_own = jnp.where(lane16 < 64, start_own // 128, start_own % 128).astype(F32).astype(BF)
+    for g in range(KVH):
+        stage[g, 2] = start_own
+    fetched = stage.at[:, pl.ds(0, 2)]
+    pltpu.make_async_copy(fetched, fetched, kv_sem).wait()
     pl.semaphore_wait(barrier, len(others))
 
     def remote(src, dst, send, recv, to):
@@ -127,13 +132,9 @@
             line_copies.append(remote(
                 stage.at[(z + d) % KVH], landed.at[at], z_send.at[d - 1], z_recv.at[wave], line[d]
             ))
-            line_copies.append(remote(
-                pos_own, pos_line.at[at], p_send.at[d - 1], p_recv.at[wave], line[d]
-            ))
     for copy in line_copies:
         copy.start()
     landed[0] = stage[head]
-    pos_line[0] = pos_own[...]
 
     q_copy.wait()
     q_over = remote(q_raw.at[0], q_raw.at[1], t_send.at[0], t_recv.at[0], twin)
@@ -161,20 +162,15 @@
     acc[...] = jnp.zeros_like(acc)
     top[...] = jnp.full_like(top, MASKED)
 
-    lane16 = lax.broadcasted_iota(jnp.int32, (TOK, 128), 1)
-
     def collect(wave):
         first = 1 - wave
-        got = pos_line.at[pl.ds(wave * HALF + first, HALF - first)]
-        pltpu.make_async_copy(got, got, p_recv.at[wave]).wait()
         got = landed.at[pl.ds(wave * HALF + first, HALF - first)]
         pltpu.make_async_copy(got, got, z_recv.at[wave]).wait()
         slot = SLOT[(0, 0, wave)]
         places = [wave * HALF + d for d in range(HALF)]
-        starts = jnp.concatenate([pos_line[d] for d in places * 2], axis=0)
-        mine[slot, BKEYS + HD:] = jnp.where(
-            lane16 < 64, starts // 128, starts % 128
-        ).astype(F32).astype(BF)
+        mine[slot, BKEYS + HD:] = jnp.concatenate(
+            [landed[d, 2].astype(F32)[0:1] for d in places * 2], axis=0
+        ).astype(BF)
         for d in range(HALF):
             mine[slot, d * TOK:(d + 1) * TOK] = landed[wave * HALF + d, 0]
         mine[slot, BKEYS:BKEYS + HD] = jnp.concatenate([landed[d, 1] for d in places], axis=0).T
@@ -194,12 +190,16 @@
     collect(0)
     pass_on(0)
 
+    def decode(word):
+        turned = pltpu.roll(word, 64, 1)
+        return jnp.where(lane16 < 64, word * 128.0 + turned, turned * 128.0 + word)
+
     lane1 = lax.broadcasted_iota(jnp.int32, (1, 128), 1)
-    token_pos = jnp.zeros((1, 128), jnp.int32)
+    token_pos = jnp.zeros((1, 128), F32)
     for cc in range(4):
+        start = decode(landed[(cc - head + HALF) % HALF, 2].astype(F32))[0:1]
         token_pos = jnp.where(
-            (lane1 % QTOK) // TOK == cc,
-            pos_line[(cc - head + HALF) % HALF] + lane1 % TOK, token_pos,
+            (lane1 % QTOK) // TOK == cc, start + (lane1 % TOK).astype(F32), token_pos
         )
     q_pos[0] = token_pos
     pos_over = remote(q_pos.at[0], q_pos.at[1], t_send.at[1], t_recv.at[1], twin)
@@ -216,14 +216,11 @@
     early = max(2, HELD[0] - 2)
     receive(1, early)
     pos_over.wait_recv()
-    limit = (
-        jnp.where(lane1 < QTOK, q_pos[0], q_pos[1]) - lax.broadcasted_iota(jnp.int32, (TOK, 128), 0)
-    ).astype(F32)
+    offset = lax.broadcasted_iota(jnp.int32, (TOK, 128), 0).astype(F32)
+    limit = jnp.where(lane1 < QTOK, q_pos[0], q_pos[1]) - offset
 
     def augmented(slot):
-        word = mine[slot, BKEYS + HD:].astype(F32)
-        turned = pltpu.roll(word, 64, 1)
-        start = jnp.where(lane16 < 64, word * 128.0 + turned, turned * 128.0 + word)
+        start = decode(mine[slot, BKEYS + HD:].astype(F32))
         bias = jnp.concatenate(
             [jnp.where(start[d:d + 1, :] <= limit, 0.0, MASKED).astype(BF) for d in range(HALF)],
             axis=0,
@@ -366,13 +363,11 @@
         out_specs=pl.BlockSpec(memory_space=pl.ANY),
         scratch_shapes=[
             pltpu.VMEM((BLOCKS, BLOCK, HD), BF),
-            pltpu.VMEM((KVH, 2, TOK, HD), BF),
-            pltpu.VMEM((NZ, 2, TOK, HD), BF),
+            pltpu.VMEM((KVH, 3, TOK, HD), BF),
+            pltpu.VMEM((NZ, 3, TOK, HD), BF),
             pltpu.SMEM((TOK,), jnp.int32),
-            pltpu.VMEM((1, 128), jnp.int32),
-            pltpu.VMEM((NZ, 1, 128), jnp.int32),
             pltpu.VMEM((2, QTOK, WIDTH), BF),
-            pltpu.VMEM((2, 1, 128), jnp.int32),
+            pltpu.VMEM((2, 1, 128), F32),
             pltpu.VMEM((ROWS, 2 * HD, 256), BF),
             pltpu.VMEM((ROWS, KEYS, 256), F32),
             pltpu.VMEM((ROWS, KEYS, 256), F32),
@@ -386,7 +381,7 @@
             pltpu.VMEM((8, 1, 256), F32),
             pltpu.VMEM((4, TOK, WIDTH), BF),
             dma, dma, dma,
-            dma((NZ - 1,)), dma((2,)), dma((NZ - 1,)), dma((2,)),
+            dma((NZ - 1,)), dma((2,)),
             dma((len(ROUTES),)), dma((BLOCKS,)), dma((2,)), dma((2,)),
             dma((8,)), dma((8,)), dma((4,)), dma((4,)),
         ],

time: 55 us -> 56.5 us (1.027)
  Pallas kernels: 53.2 us -> 54.6 us
    pallas_call x1, Pallas kernels: 53.2 us -> 54.6 us  [shards(): pl.pallas_call(kernel, out_shape=jax.ShapeDtypeStruct((TOK, KVH * WIDTH),...]
where the time goes in v2:
time: 56.5 us; the launch traced here: 56.3 us
  Pallas kernels  54.6 us (97%)
  local copies, waits for them, and re-layouts  1.67 us (3%)
    pallas_call x1, Pallas kernels, shards(): pl.pallas_call(kernel, out_shape=jax.ShapeDtypeStruct((TOK, KVH * WIDTH),...  54.6 us
    unnamed x1, local copies, waits for them, and re-layouts  1.67 us

profile of v2, /device:TPU:1, one launch (start us, length us, event | category | flops | bytes accessed | tf_op | source)
XLA Modules:
  0.0 56.3 jit_solution(12580482762304193571)
XLA Ops:
  0.0 54.6 %shard_map.46 = bf16[16,8192]{1,0:T(8,128)(2,1)} custom-call(bf16[128,8192]{1,0:T(8,128)(2,1)} %q_hbm.1, bf16[16,512]{1,0:T(8,128)(2,1)} %k_hbm.1, bf16[16,512]{1,0:T(8,128)(2,1)} %v_hbm.1, s32[16]{0:T(128)} %order_hbm.1), custom_call_target="tpu_custom_call" | custom-call | flops 4294967296 | bytes 1048576 | tf_op jit(solution)/shard_map/pallas_call | solution.py:359
  54.6 1.7 %copy.6 = bf16[16,8192]{1,0:T(8,128)(2,1)} copy(bf16[16,8192]{1,0:T(8,128)(2,1)} %shard_map.46) | data formatting | bytes 524288

commit v3 on v0

--- a/solution.py
+++ b/solution.py
@@ -105,7 +105,7 @@
     twin = device(x, y, z, 1 - core)
 
     barrier = pltpu.get_barrier_semaphore()
-    others = line[1:] + list(plane.values()) + [twin]
+    others = [line[d] for d in (1, 2, 3, 4, 12, 13, 14, 15)] + list(plane.values()) + [twin]
     for other in others:
         pl.semaphore_signal(barrier, inc=1, device_id=other, device_id_type=pl.DeviceIdType.MESH)
 
@@ -121,19 +121,30 @@
         )
 
     line_copies = []
-    for wave, ds in enumerate(([12, 13, 3, 14, 2, 15, 1], [8, 7, 9, 6, 10, 5, 11, 4])):
-        for d in ds:
-            at = wave * HALF + (NZ - d) % HALF
-            line_copies.append(remote(
-                stage.at[(z + d) % KVH], landed.at[at], z_send.at[d - 1], z_recv.at[wave], line[d]
-            ))
-            line_copies.append(remote(
-                pos_own, pos_line.at[at], p_send.at[d - 1], p_recv.at[wave], line[d]
-            ))
-    for copy in line_copies:
+    for d in (-4, -3, 3, -2, 2, -1, 1):
+        at = 3 - d
+        line_copies.append(remote(
+            stage.at[(z + d + NZ) % KVH], landed.at[at], z_send.at[at], z_recv.at[at], line[d % NZ]
+        ))
+        line_copies.append(remote(
+            pos_own, pos_line.at[at], p_send.at[at], p_recv.at[at], line[d % NZ]
+        ))
+    near_copies = list(line_copies)
+    for copy in near_copies:
         copy.start()
-    landed[0] = stage[head]
-    pos_line[0] = pos_own[...]
+    landed[3] = stage[head]
+    pos_line[3] = pos_own[...]
+
+    for first, there, to in ((0, HALF + 4, line[4]), (4, HALF, line[NZ - 4])):
+        line_copies.append(remote(
+            landed.at[pl.ds(first, 4)], landed.at[pl.ds(there, 4)],
+            z_send.at[HALF + first], z_recv.at[there], to,
+        ))
+        line_copies.append(remote(
+            pos_line.at[pl.ds(first, 4)], pos_line.at[pl.ds(there, 4)],
+            p_send.at[HALF + first], p_recv.at[there], to,
+        ))
+    far_copies = line_copies[len(near_copies):]
 
     q_copy.wait()
     q_over = remote(q_raw.at[0], q_raw.at[1], t_send.at[0], t_recv.at[0], twin)
@@ -164,11 +175,11 @@
     lane16 = lax.broadcasted_iota(jnp.int32, (TOK, 128), 1)
 
     def collect(wave):
-        first = 1 - wave
-        got = pos_line.at[pl.ds(wave * HALF + first, HALF - first)]
-        pltpu.make_async_copy(got, got, p_recv.at[wave]).wait()
-        got = landed.at[pl.ds(wave * HALF + first, HALF - first)]
-        pltpu.make_async_copy(got, got, z_recv.at[wave]).wait()
+        for copy in (near_copies, far_copies)[wave]:
+            copy.wait_recv()
+        if wave == 0:
+            for copy in far_copies:
+                copy.start()
         slot = SLOT[(0, 0, wave)]
         places = [wave * HALF + d for d in range(HALF)]
         starts = jnp.concatenate([pos_line[d] for d in places * 2], axis=0)
@@ -199,7 +210,7 @@
     for cc in range(4):
         token_pos = jnp.where(
             (lane1 % QTOK) // TOK == cc,
-            pos_line[(cc - head + HALF) % HALF] + lane1 % TOK, token_pos,
+            pos_line[cc - head + 3] + lane1 % TOK, token_pos,
         )
     q_pos[0] = token_pos
     pos_over = remote(q_pos.at[0], q_pos.at[1], t_send.at[1], t_recv.at[1], twin)
@@ -386,7 +397,7 @@
             pltpu.VMEM((8, 1, 256), F32),
             pltpu.VMEM((4, TOK, WIDTH), BF),
             dma, dma, dma,
-            dma((NZ - 1,)), dma((2,)), dma((NZ - 1,)), dma((2,)),
+            dma((NZ,)), dma((NZ,)), dma((NZ,)), dma((NZ,)),
             dma((len(ROUTES),)), dma((BLOCKS,)), dma((2,)), dma((2,)),
             dma((8,)), dma((8,)), dma((4,)), dma((4,)),
         ],

time: 55 us -> 53.2 us (0.967)
  Pallas kernels: 53.2 us -> 51.3 us
    pallas_call x1, Pallas kernels: 53.2 us -> 51.3 us  [shards(): pl.pallas_call(kernel, out_shape=jax.ShapeDtypeStruct((TOK, KVH * WIDTH),...]
where the time goes in v3:
time: 53.2 us; the launch traced here: 53 us
  Pallas kernels  51.3 us (96%)
  local copies, waits for them, and re-layouts  1.67 us (3%)
    pallas_call x1, Pallas kernels, shards(): pl.pallas_call(kernel, out_shape=jax.ShapeDtypeStruct((TOK, KVH * WIDTH),...  51.3 us
    unnamed x1, local copies, waits for them, and re-layouts  1.67 us

profile of v3, /device:TPU:1, one launch (start us, length us, event | category | flops | bytes accessed | tf_op | source)
XLA Modules:
  0.0 53.0 jit_solution(13202879194053834029)
XLA Ops:
  0.0 51.3 %shard_map.46 = bf16[16,8192]{1,0:T(8,128)(2,1)} custom-call(bf16[128,8192]{1,0:T(8,128)(2,1)} %q_hbm.1, bf16[16,512]{1,0:T(8,128)(2,1)} %k_hbm.1, bf16[16,512]{1,0:T(8,128)(2,1)} %v_hbm.1, s32[16]{0:T(128)} %order_hbm.1), custom_call_target="tpu_custom_call" | custom-call | flops 4294967296 | bytes 1048576 | tf_op jit(solution)/shard_map/pallas_call | solution.py:373
  51.3 1.7 %copy.6 = bf16[16,8192]{1,0:T(8,128)(2,1)} copy(bf16[16,8192]{1,0:T(8,128)(2,1)} %shard_map.46) | data formatting | bytes 524288

commit v4 on v3

--- a/solution.py
+++ b/solution.py
@@ -167,19 +167,22 @@
             ).astype(BF)
 
     turn(0)
-    q_over.wait_recv()
-    turn(1)
     acc[...] = jnp.zeros_like(acc)
     top[...] = jnp.full_like(top, MASKED)
 
     lane16 = lax.broadcasted_iota(jnp.int32, (TOK, 128), 1)
 
     def collect(wave):
-        for copy in (near_copies, far_copies)[wave]:
-            copy.wait_recv()
         if wave == 0:
+            for first, pairs in ((0, (2, 4, 6)), (2, (5, 3, 1, 0))):
+                for n in pairs:
+                    near_copies[2 * n].wait_recv()
+                    near_copies[2 * n + 1].wait_recv()
+                far_copies[first].start()
+                far_copies[first + 1].start()
+        else:
             for copy in far_copies:
-                copy.start()
+                copy.wait_recv()
         slot = SLOT[(0, 0, wave)]
         places = [wave * HALF + d for d in range(HALF)]
         starts = jnp.concatenate([pos_line[d] for d in places * 2], axis=0)
@@ -215,6 +218,8 @@
     q_pos[0] = token_pos
     pos_over = remote(q_pos.at[0], q_pos.at[1], t_send.at[1], t_recv.at[1], twin)
     pos_over.start()
+    q_over.wait_recv()
+    turn(1)
 
     def receive(first, last):
         for slot in range(first, last):

time: 53.2 us -> 53.3 us (level)
  no operation moved by 1% of the time
where the time goes in v4:
time: 53.3 us; the launch traced here: 53.1 us
  Pallas kernels  51.4 us (96%)
  local copies, waits for them, and re-layouts  1.67 us (3%)
    pallas_call x1, Pallas kernels, shards(): pl.pallas_call(kernel, out_shape=jax.ShapeDtypeStruct((TOK, KVH * WIDTH),...  51.4 us
    unnamed x1, local copies, waits for them, and re-layouts  1.67 us

profile of v4, /device:TPU:1, one launch (start us, length us, event | category | flops | bytes accessed | tf_op | source)
XLA Modules:
  0.0 53.1 jit_solution(7511944531357904689)
XLA Ops:
  0.0 51.4 %shard_map.46 = bf16[16,8192]{1,0:T(8,128)(2,1)} custom-call(bf16[128,8192]{1,0:T(8,128)(2,1)} %q_hbm.1, bf16[16,512]{1,0:T(8,128)(2,1)} %k_hbm.1, bf16[16,512]{1,0:T(8,128)(2,1)} %v_hbm.1, s32[16]{0:T(128)} %order_hbm.1), custom_call_target="tpu_custom_call" | custom-call | flops 4294967296 | bytes 1048576 | tf_op jit(solution)/shard_map/pallas_call | solution.py:378
  51.4 1.7 %copy.6 = bf16[16,8192]{1,0:T(8,128)(2,1)} copy(bf16[16,8192]{1,0:T(8,128)(2,1)} %shard_map.46) | data formatting | bytes 524288

commit v5 on v3

--- a/solution.py
+++ b/solution.py
@@ -374,7 +374,7 @@
         kernel,
         out_shape=jax.ShapeDtypeStruct((TOK, KVH * WIDTH), BF),
         in_specs=[pl.BlockSpec(memory_space=pl.ANY)] * 4,
-        out_specs=pl.BlockSpec(memory_space=pl.ANY),
+        out_specs=pl.BlockSpec(memory_space=pltpu.VMEM),
         scratch_shapes=[
             pltpu.VMEM((BLOCKS, BLOCK, HD), BF),
             pltpu.VMEM((KVH, 2, TOK, HD), BF),

time: 53.2 us -> 53.7 us (level)
  Pallas kernels: 51.3 us -> 51.9 us
    pallas_call x1, Pallas kernels: 51.3 us -> 51.9 us  [shards(): pl.pallas_call(kernel, out_shape=jax.ShapeDtypeStruct((TOK, KVH * WIDTH),...]
where the time goes in v5:
time: 53.7 us; the launch traced here: 53.6 us
  Pallas kernels  51.9 us (97%)
  local copies, waits for them, and re-layouts  1.67 us (3%)
    pallas_call x1, Pallas kernels, shards(): pl.pallas_call(kernel, out_shape=jax.ShapeDtypeStruct((TOK, KVH * WIDTH),...  51.9 us
    unnamed x1, local copies, waits for them, and re-layouts  1.67 us

profile of v5, /device:TPU:1, one launch (start us, length us, event | category | flops | bytes accessed | tf_op | source)
XLA Modules:
  0.0 53.6 jit_solution(9729668828760131540)
XLA Ops:
  0.0 51.9 %shard_map.46 = bf16[16,8192]{1,0:T(8,128)(2,1)} custom-call(bf16[128,8192]{1,0:T(8,128)(2,1)} %q_hbm.1, bf16[16,512]{1,0:T(8,128)(2,1)} %k_hbm.1, bf16[16,512]{1,0:T(8,128)(2,1)} %v_hbm.1, s32[16]{0:T(128)} %order_hbm.1), custom_call_target="tpu_custom_call" | custom-call | flops 4294967296 | bytes 1048576 | tf_op jit(solution)/shard_map/pallas_call | solution.py:373
  51.9 1.7 %copy.6 = bf16[16,8192]{1,0:T(8,128)(2,1)} copy(bf16[16,8192]{1,0:T(8,128)(2,1)} %shard_map.46) | data formatting | bytes 524288
